TPU v7x, 32 devices: a whole 2x2x4 slice. The times are simulated.
32 devices in a mesh: parts: 2 (over y), tensor: 4 (over z), dp: 4 (over x, core).
Axes of the slice: x: 2, y: 2, z: 4, core: 2. Of those that a mesh axis runs over, the one named last changes fastest.
Arguments:
- x_up: bfloat16 [16384, 4096], P(('parts', 'dp'), 'tensor'), parts along dimension 0, may hold values from -6 to 6
- g_up: bfloat16 [16384, 14336], P(('parts', 'dp'), 'tensor'), parts along dimension 0, may hold values from -6 to 6
- h_down: bfloat16 [16384, 14336], P(('parts', 'dp'), 'tensor'), parts along dimension 0, may hold values from -6 to 6
- g_down: bfloat16 [16384, 4096], P(('parts', 'dp'), 'tensor'), parts along dimension 0, may hold values from -6 to 6
- proj_model: bfloat16 [4096, 128], P('tensor'), may hold values from -0.09375 to 0.09375
- proj_hidden: bfloat16 [14336, 128], P('tensor'), may hold values from -0.046875 to 0.046875
- lengths: int32 [16], P(('parts', 'dp')), parts along dimension 0, may hold values from 256 to 1024, as said below
- bank: bfloat16 [1024, 8192], P(None, 'tensor'), may hold values from -2.390625 to 2.390625
Outputs:
- scores: float32 [16, 1024], P(('parts', 'dp'), 'tensor'), parts along dimension 0
There are 2 independent parts, one for each index of `parts`. A program takes and returns all parts, laid end to end along the dimension named above; an argument that names none is the same for every part. Nothing has to cross between parts.
Inputs may be any that keep to these rules, and one draw needn't show every extreme that they name: `lengths`: at least 256 live tokens in every sequence, and in every draw some sequence is entirely live.
All inputs are finite; a program needn't handle non-finite values.
Results may differ from a plain program's by a relative error of at most 0.0029.
Values sent between devices are 32-bit elements; how exact they have to be, the bound alone decides.
A program may use at most 128 MiB of HBM per device.

v0:
```python
import jax
import jax.numpy as jnp
from jax import lax
from jax.sharding import PartitionSpec as P

PROJ = 64
SEQ_LEN = 1024


def projected_rows(x_up, g_up, h_down, g_down, proj_model, proj_hidden):
    up_input = jnp.dot(x_up, proj_model[:, :PROJ], preferred_element_type=jnp.float32)
    up_output = jnp.dot(g_up, proj_hidden[:, :PROJ], preferred_element_type=jnp.float32)
    down_input = jnp.dot(h_down, proj_hidden[:, PROJ:], preferred_element_type=jnp.float32)
    down_output = jnp.dot(g_down, proj_model[:, PROJ:], preferred_element_type=jnp.float32)
    return jnp.concatenate([up_input, up_output, down_input, down_output], axis=1)


def live_weights(lengths, row_count):
    row_index = jnp.arange(row_count, dtype=jnp.int32)
    seq_index = row_index // SEQ_LEN
    position = row_index % SEQ_LEN
    seq_ids = jnp.arange(lengths.shape[0], dtype=jnp.int32)
    member = seq_index[:, None] == seq_ids[None, :]
    live_rows = position[:, None] < lengths[None, :]
    return jnp.where(member & live_rows, 1.0, 0.0).astype(jnp.float32)


def per_device(x_up, g_up, h_down, g_down, proj_model, proj_hidden, lengths, bank):
    total_rows = x_up.shape[0]
    seq_count = lengths.shape[0]
    feat_dev = bank.shape[1]
    counts = lengths.astype(jnp.float32)
    summed = lax.psum(projected_rows(x_up, g_up, h_down, g_down, proj_model, proj_hidden), "tensor")
    first_feat = lax.axis_index("tensor") * feat_dev
    square_size = PROJ * PROJ
    layer_index = first_feat // square_size
    first_input = first_feat % square_size // PROJ
    input_rows = feat_dev // PROJ
    input_cols = lax.dynamic_slice_in_dim(
        summed, layer_index * 2 * PROJ + first_input, input_rows, 1
    )
    output_cols = lax.dynamic_slice_in_dim(summed, layer_index * 2 * PROJ + PROJ, PROJ, 1)
    live_row = jnp.sum(live_weights(lengths, total_rows), axis=1)
    masked = output_cols * live_row[:, None]
    blocks = jnp.einsum(
        "spi,spj->sij",
        input_cols.reshape(seq_count, SEQ_LEN, input_rows),
        masked.reshape(seq_count, SEQ_LEN, PROJ),
        precision=lax.Precision.HIGHEST,
        preferred_element_type=jnp.float32,
    )
    features = (blocks.reshape(seq_count, feat_dev) / counts[:, None]).astype(jnp.bfloat16)
    partial_scores = lax.dot_general(
        features, bank, (((1,), (1,)), ((), ())), preferred_element_type=jnp.float32
    )
    return lax.psum_scatter(partial_scores, "tensor", scatter_dimension=1, tiled=True)


def solution(mesh):
    in_specs = (
        P(("parts", "dp"), "tensor"),
        P(("parts", "dp"), "tensor"),
        P(("parts", "dp"), "tensor"),
        P(("parts", "dp"), "tensor"),
        P("tensor", None),
        P("tensor", None),
        P(("parts", "dp")),
        P(None, "tensor"),
    )
    out_specs = P(("parts", "dp"), "tensor")
    return jax.shard_map(
        per_device, mesh=mesh, in_specs=in_specs, out_specs=out_specs, check_vma=False
    )
```

profile of v0, /device:TPU:0, one launch (start us, length us, event | category | flops | bytes accessed | tf_op | source)
XLA Modules:
  0.0 157.2 jit_solution(7162827363751485885)
XLA Ops:
  6.5 0.0 all-reduce.2.cloned.1.call-start
  6.5 10.0 %fusion = f32[2048,64]{0,1:T(8,128)S(1)} fusion(bf16[2048,3584]{1,0:T(8,128)(2,1)} %param.10, bf16[3584,128]{1,0:T(8,128)(2,1)} %param.13), kind=kOutput, calls=%fused_computation.2 | convolution fusion | flops 939524096 | bytes 16121856 | tf_op jit(solution)/shard_map/dot_general | solution.py:13
  16.6 0.0 copy-done.2
  16.6 0.0 copy-start
  16.6 0.0 copy-start.3
  16.6 9.9 %fusion.2 = f32[2048,64]{0,1:T(8,128)S(1)} fusion(bf16[2048,3584]{1,0:T(8,128)(2,1)} %param.9, bf16[3584,128]{1,0:T(8,128)(2,1)S(1)} %copy-done.2), kind=kOutput, calls=%fused_computation.4 | convolution fusion | flops 939524096 | bytes 16121856 | tf_op jit(solution)/shard_map/dot_general | solution.py:12
  26.5 0.0 copy-done.3
  26.5 0.0 copy-start.1
  26.5 1.5 fusion.9
  28.0 0.7 copy-done.1
  28.7 1.4 fusion.11
  30.1 1.5 pad_maximum_fusion
  31.6 0.0 all-reduce.2.cloned.1.call-update
  31.6 0.0 reduce-scatter.4.cloned.1.call-start
  31.8 0.1 fusion.13
  31.9 89.1 %all-reduce.2.cloned.1.call-done = f32[2048,256]{0,1:T(8,128)} async-done(((f32[2048,256]{0,1:T(8,128)}), f32[2048,256]{0,1:T(8,128)}) %all-reduce.2.cloned.1.call-update) | async-done | bytes 2097168 | tf_op jit(solution)/shard_map/psum | solution.py:33
  121.0 1.0 constant_dynamic-slice_fusion
  122.0 1.1 dynamic-slice_multiply_fusion
  123.1 0.5 fusion.4
  123.7 0.1 reshape.36
  123.8 4.3 %convolution_bitcast_fusion = f32[1024,2]{1,0:T(8,128)} fusion(bf16[1024,2048]{1,0:T(8,128)(2,1)} %param.15, f32[2,2048]{1,0:T(2,128)S(1)} %reshape.36, f32[2]{0:T(128)S(1)} %convert_element_type.6), kind=kOutput, calls=%fused_computation.1 | convolution fusion | flops 8396800 | bytes 4218888
  128.0 0.0 reduce-scatter.4.cloned.1.call-update
  128.0 20.8 %reduce-scatter.4.cloned.1.call-done = f32[256,2]{1,0:T(8,128)} async-done(((f32[1024,2]{1,0:T(8,128)}), f32[256,2]{1,0:T(8,128)}) %reduce-scatter.4.cloned.1.call-update) | async-done | bytes 2064
  148.8 1.6 copy.17
  (6 shorter events, 0.0 us)
Async XLA Ops:
  6.5 10.1 %copy-start.2 = (bf16[3584,128]{1,0:T(8,128)(2,1)S(1)}, bf16[3584,128]{1,0:T(8,128)(2,1)}, u32[]{:S(2)}) copy-start(bf16[3584,128]{1,0:T(8,128)(2,1)} %param.13) | copy-start | bytes 2752516
  6.5 114.5 %all-reduce.2.cloned.1.call-start = ((), (), s32[]{:S(2)}) async-start(), calls=%async_computation.1 | async-start | bytes 4194304 | tf_op jit(solution)/shard_map/psum | solution.py:33
  16.6 9.9 %copy-start = (bf16[2048,1024]{1,0:T(8,128)(2,1)S(1)}, bf16[2048,1024]{1,0:T(8,128)(2,1)}, u32[]{:S(2)}) copy-start(bf16[2048,1024]{1,0:T(8,128)(2,1)} %param.11) | copy-start | bytes 12582916
  16.6 9.9 %copy-start.3 = (bf16[1024,128]{1,0:T(8,128)(2,1)S(1)}, bf16[1024,128]{1,0:T(8,128)(2,1)}, u32[]{:S(2)}) copy-start(bf16[1024,128]{1,0:T(8,128)(2,1)} %param.12) | copy-start | bytes 786436
  26.5 2.2 %copy-start.1 = (bf16[2048,1024]{1,0:T(8,128)(2,1)S(1)}, bf16[2048,1024]{1,0:T(8,128)(2,1)}, u32[]{:S(2)}) copy-start(bf16[2048,1024]{1,0:T(8,128)(2,1)} %param.8) | copy-start | bytes 12582916
  30.1 1.6 %copy-start.4 = (s32[2]{0:T(128)S(1)}, s32[2]{0:T(128)}, u32[]{:S(2)}) copy-start(s32[2]{0:T(128)} %param.14) | copy-start | bytes 28
  31.6 117.2 %reduce-scatter.4.cloned.1.call-start = ((), (), s32[]{:S(2)}) async-start(), calls=%async_computation.2 | async-start | bytes 655360
Sparse Core Ops, SparseCore 0:
  31.8 89.2 all-reduce.1
  128.2 20.6 reduce-scatter.3
where the time goes:
time: 158 us; the launch traced here: 157 us
  waiting for transfers between devices  110 us (70%)
  matrix products  27.6 us (17%)
  between operations  13.6 us (9%)
  local copies, waits for them, and re-layouts  3.39 us (2%)
  other arithmetic  2.71 us (2%)
    psum x1, waiting for transfers between devices, per_device(): lax.psum(projected_rows(x_up, g_up, h_down, g_down, proj_model, proj_hidd...  89.1 us
    unnamed x3, waiting for transfers between devices  20.8 us
    dot_general x1, matrix products, projected_rows(): jnp.dot(h_down, proj_hidden[:, PROJ:], preferred_element_type=jnp.float32)  10 us
    dot_general x1, matrix products, projected_rows(): jnp.dot(g_up, proj_hidden[:, :PROJ], preferred_element_type=jnp.float32)  9.87 us
    unnamed x1, matrix products  4.26 us
  transfers between devices with their start and end apart: 2, of which 2 were waited for; matrix products, arithmetic and copies ran while one was open for 0% of the time, Pallas kernels for 0%

commit v1 on v0

v1 whole, which is shorter than its diff:
```python
import functools

import jax
import jax.numpy as jnp
from jax import lax
from jax.experimental import pallas as pl
from jax.experimental.pallas import tpu as pltpu
from jax.sharding import PartitionSpec as P

PROJ = 64
CHUNK = 64
LAG = 2
AHEAD = 3
MESH = pl.DeviceIdType.MESH


def kernel(
    n,
    x_hbm, g_hbm, h_hbm, d_hbm, pm_hbm, ph_hbm, len_ref, bank_hbm,
    out_ref,
    xb, gb, hb, db, pm, ph, bank,
    own, got, acc, feat_out, feat_in, flat, part, part_in,
    row_sem, map_sem, send_sem, recv_sem, feat_send, feat_recv, part_send, part_recv,
):
    me = lax.axis_index("tensor")
    left, right = lax.rem(me + n - 1, n), lax.rem(me + 1, n)
    half = x_hbm.shape[0] // 2
    chunks = half // CHUNK
    queries = bank_hbm.shape[0] // n

    barrier = pltpu.get_barrier_semaphore()
    for j in range(1, n):
        pl.semaphore_signal(
            barrier, inc=1, device_id={"tensor": lax.rem(me + j, n)}, device_id_type=MESH
        )

    pairs = ((x_hbm, xb), (g_hbm, gb), (h_hbm, hb), (d_hbm, db))

    def row_copy(a, side, s):
        src, dst = pairs[a]
        return pltpu.make_async_copy(
            src.at[pl.ds(side * half + s * CHUNK, CHUNK)],
            dst.at[s, pl.ds(side * CHUNK, CHUNK)],
            row_sem.at[2 * a + side, s],
        )

    def fetch(s):
        for a in range(4):
            for side in range(2):
                row_copy(a, side, s).start()

    pm_copy = pltpu.make_async_copy(pm_hbm, pm, map_sem.at[0])
    ph_copy = pltpu.make_async_copy(ph_hbm, ph, map_sem.at[1])
    bank_copy = pltpu.make_async_copy(bank_hbm, bank, map_sem.at[2])
    pm_copy.start()
    ph_copy.start()
    for s in range(AHEAD):
        fetch(s)
    acc[...] = jnp.zeros_like(acc)
    flat[...] = jnp.zeros_like(flat)
    pl.semaphore_wait(barrier, n - 1)
    pm_copy.wait()
    ph_copy.wait()

    def chain_copy(side, k):
        return pltpu.make_async_remote_copy(
            src_ref=own.at[side, k],
            dst_ref=got.at[side, k],
            send_sem=send_sem.at[side, k],
            recv_sem=recv_sem.at[side, k],
            device_id={"tensor": left if side == 0 else right},
            device_id_type=MESH,
        )

    first = (n - 1, 0)
    last = (0, n - 1)
    lags = ((n - 1 - me) * LAG, me * LAG)

    def outer(side, k):
        both = own[side, k]
        position = k * CHUNK + lax.broadcasted_iota(jnp.int32, (CHUNK, 128), 0)
        outputs = jnp.where(position < len_ref[side], both[:, 128:], 0.0)
        acc[...] += lax.dot_general(
            both[:, :128], outputs, (((0,), (0,)), ((), ())),
            precision=lax.Precision.HIGHEST, preferred_element_type=jnp.float32,
        )

    def step(s, carry):
        @pl.when(s + AHEAD < chunks)
        def _():
            fetch(s + AHEAD)

        @pl.when(s == chunks - AHEAD)
        def _():
            bank_copy.start()

        @pl.when(s < chunks)
        def _():
            for a in range(4):
                for side in range(2):
                    row_copy(a, side, s).wait()
            low = lax.broadcasted_iota(jnp.int32, (2 * CHUNK, 128), 1) < PROJ
            dot = functools.partial(jnp.dot, preferred_element_type=jnp.float32)
            inputs = jnp.where(low, dot(xb[s], pm[...]), dot(hb[s], ph[...]))
            outputs = jnp.where(low, dot(gb[s], ph[...]), dot(db[s], pm[...]))
            for side in range(2):
                rows = slice(side * CHUNK, (side + 1) * CHUNK)
                own[side, s, :, :128] = inputs[rows]
                own[side, s, :, 128:] = outputs[rows]

                @pl.when(me == first[side])
                def _():
                    chain_copy(side, s).start()

        for side in range(2):
            k = s - lags[side]

            @pl.when((k >= 0) & (k < chunks) & (me != first[side]))
            def _():
                chain_copy(side, k).wait_recv()
                own[side, k] = own[side, k] + got[side, k]

                @pl.when(me != last[side])
                def _():
                    chain_copy(side, k).start()

                @pl.when(me == last[side])
                def _():
                    outer(side, k)

        return carry

    lax.fori_loop(0, chunks + (n - 1) * LAG, step, 0)

    def feat_copy(side, t):
        return pltpu.make_async_remote_copy(
            src_ref=feat_out.at[t],
            dst_ref=feat_in.at[side],
            send_sem=feat_send.at[t],
            recv_sem=feat_recv.at[side],
            device_id={"tensor": t},
            device_id_type=MESH,
        )

    rows = feat_out.shape[1]
    for side in range(2):
        @pl.when(me == last[side])
        def _():
            count = len_ref[side].astype(jnp.float32)
            even = acc[pl.ds(0, PROJ, stride=2), :]
            odd = acc[pl.ds(1, PROJ, stride=2), :]
            low = lax.broadcasted_iota(jnp.int32, (PROJ // 2, 128), 1) < PROJ
            up = jnp.where(low, even[: PROJ // 2], pltpu.roll(odd, PROJ, 1)[: PROJ // 2])
            down = jnp.where(low, pltpu.roll(even, PROJ, 1)[PROJ // 2 :], odd[PROJ // 2 :])
            features = jnp.concatenate([up, down], axis=0) / count
            for t in range(n):
                feat_out[t] = features[t * rows : (t + 1) * rows]
            for t in range(n):
                if t != last[side]:
                    feat_copy(side, t).start()
            feat_in[side] = feat_out[last[side]]

        @pl.when(me != last[side])
        def _():
            feat_copy(side, me).wait_recv()

    for side in range(2):
        for r in range(rows):
            flat[side : side + 1, r * 128 : (r + 1) * 128] = feat_in[side, r : r + 1, :]
    features = flat[...].astype(jnp.bfloat16)
    bank_copy.wait()

    def part_copy(j):
        t = lax.rem(me + j, n)
        return pltpu.make_async_remote_copy(
            src_ref=part.at[t],
            dst_ref=part_in.at[me],
            send_sem=part_send.at[j],
            recv_sem=part_recv.at[me],
            device_id={"tensor": t},
            device_id_type=MESH,
        )

    for j in [*range(1, n), 0]:
        t = lax.rem(me + j, n)
        scores = lax.dot_general(
            bank[pl.ds(pl.multiple_of(t * queries, queries), queries), :], features,
            (((1,), (1,)), ((), ())), preferred_element_type=jnp.float32,
        )
        part[t] = scores.T
        if j:
            part_copy(j).start()
    total = part[me]
    for j in range(1, n):
        source = lax.rem(me + j, n)
        pltpu.make_async_remote_copy(
            src_ref=part.at[source],
            dst_ref=part_in.at[source],
            send_sem=part_send.at[j],
            recv_sem=part_recv.at[source],
            device_id={"tensor": source},
            device_id_type=MESH,
        ).wait_recv()
        total = total + part_in[source]
    out_ref[...] = total[: out_ref.shape[0]]

    for side in range(2):
        @pl.when(me != last[side])
        def _():
            def sent(k, carry):
                chain_copy(side, k).wait_send()
                return carry

            lax.fori_loop(0, chunks, sent, 0)

        @pl.when(me == last[side])
        def _():
            for t in range(n):
                if t != last[side]:
                    feat_copy(side, t).wait_send()
    for j in range(1, n):
        part_copy(j).wait_send()


def per_device(n, x_up, g_up, h_down, g_down, proj_model, proj_hidden, lengths, bank):
    chunks = x_up.shape[0] // (2 * CHUNK)
    nq, feat_dev = bank.shape
    bf16, f32 = jnp.bfloat16, jnp.float32
    dma = pltpu.SemaphoreType.DMA
    hbm = pl.BlockSpec(memory_space=pl.ANY)
    tall = 2 * CHUNK
    return pl.pallas_call(
        functools.partial(kernel, n),
        out_shape=jax.ShapeDtypeStruct((lengths.shape[0], nq // n), f32),
        in_specs=[hbm] * 6 + [pl.BlockSpec(memory_space=pltpu.SMEM), hbm],
        out_specs=pl.BlockSpec(memory_space=pltpu.VMEM),
        scratch_shapes=[
            pltpu.VMEM((chunks, tall, x_up.shape[1]), bf16),
            pltpu.VMEM((chunks, tall, g_up.shape[1]), bf16),
            pltpu.VMEM((chunks, tall, h_down.shape[1]), bf16),
            pltpu.VMEM((chunks, tall, g_down.shape[1]), bf16),
            pltpu.VMEM(proj_model.shape, bf16),
            pltpu.VMEM(proj_hidden.shape, bf16),
            pltpu.VMEM(bank.shape, bf16),
            pltpu.VMEM((2, chunks, CHUNK, 256), f32),
            pltpu.VMEM((2, chunks, CHUNK, 256), f32),
            pltpu.VMEM((128, 128), f32),
            pltpu.VMEM((n, feat_dev // 128, 128), f32),
            pltpu.VMEM((2, feat_dev // 128, 128), f32),
            pltpu.VMEM((8, feat_dev), f32),
            pltpu.VMEM((n, 8, nq // n), f32),
            pltpu.VMEM((n, 8, nq // n), f32),
            dma((8, chunks)),
            dma((3,)),
            dma((2, chunks)),
            dma((2, chunks)),
            dma((n,)),
            dma((2,)),
            dma((n,)),
            dma((n,)),
        ],
        compiler_params=pltpu.CompilerParams(
            collective_id=0, has_side_effects=True, vmem_limit_bytes=58 * 1024 * 1024
        ),
        name="grad_scores",
    )(x_up, g_up, h_down, g_down, proj_model, proj_hidden, lengths, bank)


def solution(mesh):
    in_specs = (
        P(("parts", "dp"), "tensor"),
        P(("parts", "dp"), "tensor"),
        P(("parts", "dp"), "tensor"),
        P(("parts", "dp"), "tensor"),
        P("tensor", None),
        P("tensor", None),
        P(("parts", "dp")),
        P(None, "tensor"),
    )
    return jax.shard_map(
        functools.partial(per_device, mesh.shape["tensor"]),
        mesh=mesh,
        in_specs=in_specs,
        out_specs=P(("parts", "dp"), "tensor"),
        check_vma=False,
    )
```

time: 158 us -> 59.9 us (0.38)
  waiting for transfers between devices: 110 us -> 0 us
  Pallas kernels: 0 us -> 58.4 us
  matrix products: 27.6 us -> 0 us
  between operations: 13.6 us -> 0.01 us
  other arithmetic: 2.71 us -> 0 us
  local copies, waits for them, and re-layouts: 3.39 us -> 1.26 us
    psum x1 -> x0, waiting for transfers between devices: 89.1 us -> none  [per_device(): lax.psum(projected_rows(x_up, g_up, h_down, g_down, proj_model, proj_hidd...]
    pallas_call x0 -> x1, Pallas kernels: none -> 58.4 us  [per_device(): pl.pallas_call(functools.partial(kernel, n), out_shape=jax.ShapeDtypeStru...]
    dot_general x5 -> x0, matrix products: 23.3 us -> none  [the longest x1 10 us: projected_rows(): jnp.dot(h_down, proj_hidden[:, PROJ:], preferred_element_type=jnp.float32)]
    unnamed x3 -> x0, waiting for transfers between devices: 20.8 us -> none
    unnamed x1 -> x0, matrix products: 4.26 us -> none
  transfers between devices with their start and end apart: 2 -> 0, of which waited for: 2 -> 0; matrix products, arithmetic and copies ran while one was open for 0% -> 0% of each run, Pallas kernels for 0% -> 0%
where the time goes in v1:
time: 59.9 us; the launch traced here: 59.7 us
  Pallas kernels  58.4 us (97%)
  local copies, waits for them, and re-layouts  1.26 us (2%)
    pallas_call x1, Pallas kernels, per_device(): pl.pallas_call(functools.partial(kernel, n), out_shape=jax.ShapeDtypeStru...  58.4 us
    unnamed x1, local copies, waits for them, and re-layouts  1.26 us

profile of v1, /device:TPU:0, one launch (start us, length us, event | category | flops | bytes accessed | tf_op | source)
XLA Modules:
  0.0 59.7 jit_solution(14102489741026130742)
XLA Ops:
  0.0 58.4 %grad_scores.1 = f32[2,256]{1,0:T(2,128)} custom-call(bf16[2048,1024]{1,0:T(8,128)(2,1)} %x_hbm.1, bf16[2048,3584]{1,0:T(8,128)(2,1)} %g_hbm.1, bf16[2048,3584]{1,0:T(8,128)(2,1)} %h_hbm.1, bf16[2048,1024]{1,0:T(8,128)(2,1)} %d_hbm.1, bf16[1024,128]{1,0:T(8,128)(2,1)} %pm_hbm.1, bf16[3584,128]{1,0:T(8,128)(2,1)} %ph_hbm.1, s32[2]{0:T(128)} %len_ref.1, ...), custom_call_target="tpu_custom_call" | custom-call | tf_op jit(solution)/shard_map/grad_scores/pallas_call | solution.py:232
  58.4 1.3 %copy.10 = f32[2,256]{1,0:T(2,128)} copy(f32[2,256]{1,0:T(2,128)} %grad_scores.1) | data formatting | bytes 4096

commit v2 on v1

--- a/solution.py
+++ b/solution.py
@@ -9,7 +9,7 @@
 
 PROJ = 64
 CHUNK = 64
-LAG = 2
+LAG = 3
 AHEAD = 3
 MESH = pl.DeviceIdType.MESH
 

time: 59.9 us -> 55 us (0.918)
  Pallas kernels: 58.4 us -> 53.5 us
    pallas_call x1, Pallas kernels: 58.4 us -> 53.5 us  [per_device(): pl.pallas_call(functools.partial(kernel, n), out_shape=jax.ShapeDtypeStru...]
where the time goes in v2:
time: 55 us; the launch traced here: 54.8 us
  Pallas kernels  53.5 us (97%)
  local copies, waits for them, and re-layouts  1.26 us (2%)
    pallas_call x1, Pallas kernels, per_device(): pl.pallas_call(functools.partial(kernel, n), out_shape=jax.ShapeDtypeStru...  53.5 us
    unnamed x1, local copies, waits for them, and re-layouts  1.26 us

profile of v2, /device:TPU:0, one launch (start us, length us, event | category | flops | bytes accessed | tf_op | source)
XLA Modules:
  0.0 54.8 jit_solution(12278585879745767465)
XLA Ops:
  0.0 53.5 %grad_scores.1 = f32[2,256]{1,0:T(2,128)} custom-call(bf16[2048,1024]{1,0:T(8,128)(2,1)} %x_hbm.1, bf16[2048,3584]{1,0:T(8,128)(2,1)} %g_hbm.1, bf16[2048,3584]{1,0:T(8,128)(2,1)} %h_hbm.1, bf16[2048,1024]{1,0:T(8,128)(2,1)} %d_hbm.1, bf16[1024,128]{1,0:T(8,128)(2,1)} %pm_hbm.1, bf16[3584,128]{1,0:T(8,128)(2,1)} %ph_hbm.1, s32[2]{0:T(128)} %len_ref.1, ...), custom_call_target="tpu_custom_call" | custom-call | tf_op jit(solution)/shard_map/grad_scores/pallas_call | solution.py:232
  53.5 1.3 %copy.10 = f32[2,256]{1,0:T(2,128)} copy(f32[2,256]{1,0:T(2,128)} %grad_scores.1) | data formatting | bytes 4096

commit v3 on v2

--- a/solution.py
+++ b/solution.py
@@ -10,7 +10,7 @@
 PROJ = 64
 CHUNK = 64
 LAG = 3
-AHEAD = 3
+AHEAD = 2
 MESH = pl.DeviceIdType.MESH
 
 

time: 55 us -> 54.3 us (0.987)
  Pallas kernels: 53.5 us -> 52.8 us
    pallas_call x1, Pallas kernels: 53.5 us -> 52.8 us  [per_device(): pl.pallas_call(functools.partial(kernel, n), out_shape=jax.ShapeDtypeStru...]
where the time goes in v3:
time: 54.3 us; the launch traced here: 54.1 us
  Pallas kernels  52.8 us (97%)
  local copies, waits for them, and re-layouts  1.26 us (2%)
    pallas_call x1, Pallas kernels, per_device(): pl.pallas_call(functools.partial(kernel, n), out_shape=jax.ShapeDtypeStru...  52.8 us
    unnamed x1, local copies, waits for them, and re-layouts  1.26 us

profile of v3, /device:TPU:0, one launch (start us, length us, event | category | flops | bytes accessed | tf_op | source)
XLA Modules:
  0.0 54.1 jit_solution(8638439548852700063)
XLA Ops:
  0.0 52.8 %grad_scores.1 = f32[2,256]{1,0:T(2,128)} custom-call(bf16[2048,1024]{1,0:T(8,128)(2,1)} %x_hbm.1, bf16[2048,3584]{1,0:T(8,128)(2,1)} %g_hbm.1, bf16[2048,3584]{1,0:T(8,128)(2,1)} %h_hbm.1, bf16[2048,1024]{1,0:T(8,128)(2,1)} %d_hbm.1, bf16[1024,128]{1,0:T(8,128)(2,1)} %pm_hbm.1, bf16[3584,128]{1,0:T(8,128)(2,1)} %ph_hbm.1, s32[2]{0:T(128)} %len_ref.1, ...), custom_call_target="tpu_custom_call" | custom-call | tf_op jit(solution)/shard_map/grad_scores/pallas_call | solution.py:232
  52.8 1.3 %copy.10 = f32[2,256]{1,0:T(2,128)} copy(f32[2,256]{1,0:T(2,128)} %grad_scores.1) | data formatting | bytes 4096
